TPU v7x, 32 devices: a whole 2x2x4 slice. The times are simulated.
32 devices in a mesh: group: 4 (over y, x), tp: 8 (over z, core).
Axes of the slice: x: 2, y: 2, z: 4, core: 2. Of those that a mesh axis runs over, the one named last changes fastest.
Arguments:
- decoding_input: bfloat16 [8, 8, 5120], P('group'), may hold values from -6 to 6
- query_weight: bfloat16 [5120, 1024], P(None, 'tp'), may hold values from -0.078125 to 0.078125
- output_weight: bfloat16 [1024, 5120], P('tp'), may hold values from -0.25 to 0.25
- query_down_factor: bfloat16 [5120, 64], P('tp', 'group'), may hold values from -0.078125 to 0.078125
- query_up_factor: bfloat16 [64, 1024], P('group', 'tp'), may hold values from -0.75 to 0.75
- output_down_factor: bfloat16 [1024, 64], P('tp', 'group'), may hold values from -0.1875 to 0.1875
- output_up_factor: bfloat16 [64, 5120], P('group', 'tp'), may hold values from -0.75 to 0.75
- stored_keys: bfloat16 [8, 1, 2048, 128], P('group', None, 'tp')
- stored_values: bfloat16 [8, 1, 2048, 128], P('group', None, 'tp'), may hold values from -96 to 96
- current_keys: bfloat16 [8, 8, 1, 128], P('group'), may hold values from -6 to 6
- current_values: bfloat16 [8, 8, 1, 128], P('group'), may hold values from -96 to 96
- lengths: int32 [8], P('group'), may hold values from 1 to 2048, 8192 in all
Outputs:
- attended: bfloat16 [8, 8, 5120], P('group', None, 'tp')
All inputs are finite; a program needn't handle non-finite values. No bound on the sum of `lengths` on one device may be relied on, other than what follows from the above.
Results may differ from a plain program's by a relative error of at most 0.0085.
The roundings to bfloat16 on the way count: a program that leaves them out, or rounds other values in their place, can miss the bound.
Values may be sent and summed in bfloat16 or wider, within the bound.
A program may use at most 64 MiB of HBM per device.

v0:
```python
import jax
import jax.numpy as jnp
from jax import lax
from jax.sharding import PartitionSpec as P

adapter_scale = 2.0
masked_score = -1e30
highest_precision = lax.Precision.HIGHEST


def joined(value, axis, join):
    pieces = jax.tree.map(lambda part: lax.all_gather(part, axis), value)
    head = jax.tree.map(lambda part: part[0], pieces)
    tail = jax.tree.map(lambda part: part[1:], pieces)
    so_far, _ = lax.scan(lambda so_far, section: (join(so_far, section), None), head, tail)
    return so_far


def join_states(state_one, state_two):
    joint_peak = jnp.maximum(state_one[0], state_two[0])
    left = jnp.exp(state_one[0] - joint_peak)
    right = jnp.exp(state_two[0] - joint_peak)
    return (
        joint_peak,
        state_one[1] * left + state_two[1] * right,
        state_one[2] * left[..., None] + state_two[2] * right[..., None],
    )


def on_device(
    decoding_input,
    query_weight,
    output_weight,
    query_down_factor,
    query_up_factor,
    output_down_factor,
    output_up_factor,
    stored_keys,
    stored_values,
    current_keys,
    current_values,
    lengths,
):
    tp_count = lax.axis_size("tp")
    tp_index = lax.axis_index("tp")
    row_count, step_count, model_width = decoding_input.shape
    kv_heads = stored_keys.shape[1]
    block_size = stored_keys.shape[2]
    head_size = stored_keys.shape[3]
    heads_here = query_weight.shape[1] // head_size
    head_count = heads_here * tp_count
    group_heads = head_count // kv_heads
    slice_width = model_width // tp_count
    flattened_input = decoding_input.reshape(row_count * step_count, model_width)
    qa_part, query_up_columns, oa_rows, ob_part = (
        lax.all_gather(query_down_factor, "group", axis=1, tiled=True),
        lax.all_gather(query_up_factor, "group", axis=0, tiled=True),
        lax.all_gather(output_down_factor, "group", axis=1, tiled=True),
        lax.all_gather(output_up_factor, "group", axis=0, tiled=True),
    )
    qa_whole, ob_whole = (
        lax.all_gather(qa_part, "tp", axis=0, tiled=True),
        lax.all_gather(ob_part, "tp", axis=1, tiled=True),
    )
    adapter_rank_input = jnp.dot(flattened_input, qa_whole, preferred_element_type=jnp.float32)
    query_rows = jnp.dot(
        flattened_input, query_weight, preferred_element_type=jnp.float32
    ) + adapter_scale * jnp.dot(
        adapter_rank_input, query_up_columns.astype(jnp.float32), precision=highest_precision
    )
    query_rows = query_rows.astype(jnp.bfloat16).reshape(
        row_count, step_count, heads_here, head_size
    )
    all_queries = lax.all_gather(query_rows, "tp", axis=2, tiled=True)
    grouped = all_queries.reshape(row_count, step_count, kv_heads, group_heads, head_size)
    score_scale = head_size ** (-0.5)
    scores = (
        jnp.einsum("rskgd,rkcd->rskgc", grouped, stored_keys, preferred_element_type=jnp.float32)
        * score_scale
    )
    position = tp_index * block_size + lax.iota(jnp.int32, block_size)
    visible = (position[None, :] < lengths[:, None])[:, None, None, None, :]
    peaks = jnp.max(jnp.where(visible, scores, masked_score), axis=-1)
    weights = jnp.where(visible, jnp.exp(scores - peaks[..., None]), 0.0)
    weight_sums = jnp.sum(weights, axis=-1)
    outputs = jnp.einsum(
        "rskgc,rkcd->rskgd",
        weights.astype(jnp.bfloat16),
        stored_values,
        preferred_element_type=jnp.float32,
    )
    peaks = peaks.reshape(row_count, step_count, head_count)
    weight_sums = weight_sums.reshape(row_count, step_count, head_count)
    outputs = outputs.reshape(row_count, step_count, head_count, head_size)
    head_start = tp_index * heads_here
    peaks, weight_sums, outputs = joined((peaks, weight_sums, outputs), "tp", join_states)
    cache_peak = lax.dynamic_slice_in_dim(peaks, head_start, heads_here, 2)
    cache_sum = lax.dynamic_slice_in_dim(weight_sums, head_start, heads_here, 2)
    cache_out = lax.dynamic_slice_in_dim(outputs, head_start, heads_here, 2)
    shared_head = head_start // group_heads
    fresh_keys = lax.dynamic_slice_in_dim(current_keys, shared_head, 1, 2)[:, :, 0, :]
    fresh_values = lax.dynamic_slice_in_dim(current_values, shared_head, 1, 2)[:, :, 0, :]
    fresh_scores = (
        jnp.einsum("rshd,rtd->rsht", query_rows, fresh_keys, preferred_element_type=jnp.float32)
        * score_scale
    )
    order = lax.iota(jnp.int32, step_count)
    causal = (order[:, None] >= order[None, :])[None, :, None, :]
    fresh_peak = jnp.max(jnp.where(causal, fresh_scores, masked_score), axis=-1)
    fresh_weights = jnp.where(causal, jnp.exp(fresh_scores - fresh_peak[..., None]), 0.0)
    fresh_sum = jnp.sum(fresh_weights, axis=-1)
    fresh_out = jnp.einsum(
        "rsht,rtd->rshd",
        fresh_weights.astype(jnp.bfloat16),
        fresh_values,
        preferred_element_type=jnp.float32,
    )
    joint_peak = jnp.maximum(cache_peak, fresh_peak)
    left = jnp.exp(cache_peak - joint_peak)
    right = jnp.exp(fresh_peak - joint_peak)
    numer = cache_out * left[..., None] + fresh_out * right[..., None]
    denom = cache_sum * left + fresh_sum * right
    context_rows = (
        (numer / denom[..., None])
        .astype(jnp.bfloat16)
        .reshape(row_count * step_count, heads_here * head_size)
    )
    partial_output_value = jnp.dot(context_rows, output_weight, preferred_element_type=jnp.float32)
    adapter_rank_output = jnp.dot(context_rows, oa_rows, preferred_element_type=jnp.float32)
    partial_output_value = partial_output_value + adapter_scale * jnp.dot(
        adapter_rank_output, ob_whole.astype(jnp.float32), precision=highest_precision
    )
    summed_whole = lax.psum(partial_output_value, "tp")
    result = lax.dynamic_slice_in_dim(summed_whole, tp_index * slice_width, slice_width, 1)
    return result.astype(jnp.bfloat16).reshape(row_count, step_count, slice_width)


def solution(mesh):
    in_specs = (
        P("group", None, None),
        P(None, "tp"),
        P("tp", None),
        P("tp", "group"),
        P("group", "tp"),
        P("tp", "group"),
        P("group", "tp"),
        P("group", None, "tp", None),
        P("group", None, "tp", None),
        P("group", None, None, None),
        P("group", None, None, None),
        P("group"),
    )
    out_specs = P("group", None, "tp")
    return jax.shard_map(
        on_device, mesh=mesh, in_specs=in_specs, out_specs=out_specs, check_vma=False
    )
```

profile of v0, /device:TPU:0, one launch (start us, length us, event | category | flops | bytes accessed | tf_op | source)
XLA Modules:
  0.0 160.9 jit_solution(3426879444370139693)
XLA Ops:
  0.0 0.9 broadcast_compare_fusion
  0.9 10.0 %all_gather.30 = bf16[640,64]{0,1:T(8,128)(2,1)S(1)} all-gather(bf16[640,16]{0,1:T(8,128)(2,1)} %param.17), channel_id=1, replica_groups=mesh['group'=4,'tp'=8] {'group'}, dimensions={1}, use_global_device_ids=true | all-gather | bytes 102400 | tf_op jit(solution)/shard_map/all_gather | solution.py:56
  10.9 15.8 %all_gather.31 = bf16[5120,64]{0,1:T(8,128)(2,1)S(1)} all-gather(bf16[640,64]{0,1:T(8,128)(2,1)S(1)} %all_gather.30), channel_id=1, replica_groups=mesh['group'=4,'tp'=8] {'tp'}, dimensions={0}, use_global_device_ids=true | all-gather | bytes 737280 | tf_op jit(solution)/shard_map/all_gather | solution.py:62
  26.7 1.2 fusion.10
  28.0 8.1 %all_gather.32 = bf16[64,128]{1,0:T(8,128)(2,1)S(1)} all-gather(bf16[16,128]{1,0:T(8,128)(2,1)S(1)} %copy-done.6), channel_id=1, replica_groups=mesh['group'=4,'tp'=8] {'group'}, dimensions={0}, use_global_device_ids=true | all-gather | bytes 20480 | tf_op jit(solution)/shard_map/all_gather | solution.py:57
  36.1 0.1 convolution_multiply_fusion.4
  36.2 0.3 fusion.7
  36.5 14.0 %all_gather.33 = bf16[2,8,8,128]{3,1,0,2:T(8,128)(2,1)S(1)} all-gather(bf16[2,8,1,128]{3,1,0,2:T(8,128)(2,1)S(1)} %bitcast.128), channel_id=1, replica_groups=mesh['group'=4,'tp'=8] {'tp'}, dimensions={2}, use_global_device_ids=true | all-gather | bytes 36864 | tf_op jit(solution)/shard_map/all_gather | solution.py:74
  50.5 0.3 select_reduce_fusion
  50.8 14.0 %all-gather = f32[16,8,8]{2,1,0:T(8,128)S(1)} all-gather(f32[2,8,8]{2,1,0:T(8,128)S(1)} %get-tuple-element.68), channel_id=2, replica_groups=mesh['group'=4,'tp'=8] {'tp'}, dimensions={0}, use_global_device_ids=true | all-gather | bytes 4608 | tf_op jit(solution)/shard_map/all_gather | solution.py:12
  64.7 0.2 bitcast_reduce_fusion
  64.9 14.0 %all-gather.1 = f32[16,8,8]{2,1,0:T(8,128)S(1)} all-gather(f32[2,8,8]{2,1,0:T(8,128)S(1)} %bitcast_reduce_fusion), channel_id=3, replica_groups=mesh['group'=4,'tp'=8] {'tp'}, dimensions={0}, use_global_device_ids=true | all-gather | bytes 4608 | tf_op jit(solution)/shard_map/all_gather | solution.py:12
  78.9 0.2 convolution_bitcast_fusion
  79.1 14.7 %all-gather.2 = f32[16,8,1,8,128]{4,3,2,1,0:T(8,128)S(1)} all-gather(f32[2,8,1,8,128]{4,3,2,1,0:T(8,128)S(1)} %convolution_bitcast_fusion), channel_id=4, replica_groups=mesh['group'=4,'tp'=8] {'tp'}, dimensions={0}, use_global_device_ids=true | all-gather | bytes 589824 | tf_op jit(solution)/shard_map/all_gather | solution.py:12
  93.9 1.1 while.14
  95.1 0.1 select_reduce_fusion.1
  95.4 0.1 fusion.9
  95.6 7.4 %all_gather.37 = bf16[128,64]{0,1:T(8,128)(2,1)S(1)} all-gather(bf16[128,16]{0,1:T(8,128)(2,1)S(1)} %copy-done.7), channel_id=1, replica_groups=mesh['group'=4,'tp'=8] {'group'}, dimensions={1}, use_global_device_ids=true | all-gather | bytes 20480 | tf_op jit(solution)/shard_map/all_gather | solution.py:58
  103.1 8.2 %all_gather.38 = bf16[64,640]{1,0:T(8,128)(2,1)S(1)} all-gather(bf16[16,640]{1,0:T(8,128)(2,1)S(1)} %copy-done.5), channel_id=1, replica_groups=mesh['group'=4,'tp'=8] {'group'}, dimensions={0}, use_global_device_ids=true | all-gather | bytes 102400 | tf_op jit(solution)/shard_map/all_gather | solution.py:59
  111.3 15.6 %all_gather.39 = bf16[64,5120]{1,0:T(8,128)(2,1)S(1)} all-gather(bf16[64,640]{1,0:T(8,128)(2,1)S(1)} %all_gather.38), channel_id=1, replica_groups=mesh['group'=4,'tp'=8] {'tp'}, dimensions={1}, use_global_device_ids=true | all-gather | bytes 737280 | tf_op jit(solution)/shard_map/all_gather | solution.py:63
  126.9 0.4 convolution_multiply_fusion
  127.3 0.3 convolution_add_fusion
  127.6 32.7 %all-reduce.1 = bf16[16,5120]{1,0:T(8,128)(2,1)S(1)} all-reduce(f32[16,5120]{1,0:T(8,128)S(1)} %convolution_add_fusion), channel_id=1, replica_groups=mesh['group'=4,'tp'=8] {'tp'}, use_global_device_ids=true, to_apply=%region_6.7 | all-reduce | flops 81920 | bytes 491520 | tf_op jit(solution)/shard_map/psum | solution.py:133
  160.3 0.6 fusion.21
  (48 shorter events, 1.4 us)
Async XLA Ops:
  0.0 127.3 %copy-start = (bf16[128,5120]{1,0:T(8,128)(2,1)S(1)}, bf16[128,5120]{1,0:T(8,128)(2,1)}, u32[]{:S(2)}) copy-start(bf16[128,5120]{1,0:T(8,128)(2,1)} %param.16) | copy-start | bytes 3932164
  0.0 36.2 %copy-start.2 = (bf16[2,8,5120]{2,1,0:T(8,128)(2,1)S(1)}, bf16[2,8,5120]{2,1,0:T(8,128)(2,1)}, u32[]{:S(2)}) copy-start(bf16[2,8,5120]{2,1,0:T(8,128)(2,1)} %param.14) | copy-start | bytes 491524
  0.0 27.9 %copy-start.6 = (bf16[16,128]{1,0:T(8,128)(2,1)S(1)}, bf16[16,128]{1,0:T(8,128)(2,1)}, u32[]{:S(2)}) copy-start(bf16[16,128]{1,0:T(8,128)(2,1)} %param.18) | copy-start | bytes 12292
  0.0 36.2 %copy-start.1 = (bf16[5120,128]{1,0:T(8,128)(2,1)S(1)}, bf16[5120,128]{1,0:T(8,128)(2,1)}, u32[]{:S(2)}) copy-start(bf16[5120,128]{1,0:T(8,128)(2,1)} %param.15) | copy-start | bytes 3932164
  26.7 23.8 %copy-start.3 = (bf16[2,1,256,128]{3,2,1,0:T(8,128)(2,1)S(1)}, bf16[2,1,256,128]{3,2,1,0:T(8,128)(2,1)}, u32[]{:S(2)}) copy-start(bf16[2,1,256,128]{3,2,1,0:T(8,128)(2,1)} %param.21) | copy-start | bytes 393220
  28.0 50.9 %copy-start.4 = (bf16[2,1,256,128]{3,2,1,0:T(8,128)(2,1)S(1)}, bf16[2,1,256,128]{3,2,1,0:T(8,128)(2,1)}, u32[]{:S(2)}) copy-start(bf16[2,1,256,128]{3,2,1,0:T(8,128)(2,1)} %param.22) | copy-start | bytes 393220
  93.9 1.3 copy-start.8
  93.9 1.6 copy-start.9
  93.9 1.7 %copy-start.7 = (bf16[128,16]{0,1:T(8,128)(2,1)S(1)}, bf16[128,16]{0,1:T(8,128)(2,1)}, u32[]{:S(2)}) copy-start(bf16[128,16]{0,1:T(8,128)(2,1)} %param.19) | copy-start | bytes 12292
  93.9 9.2 %copy-start.5 = (bf16[16,640]{1,0:T(8,128)(2,1)S(1)}, bf16[16,640]{1,0:T(8,128)(2,1)}, u32[]{:S(2)}) copy-start(bf16[16,640]{1,0:T(8,128)(2,1)} %param.20) | copy-start | bytes 61444
where the time goes:
time: 161 us
  blocking collectives  154 us (96%)
  matrix products  3.16 us (2%)
  other arithmetic  2.03 us (1%)
    all_gather x3, blocking collectives, joined(): pieces = jax.tree.map(lambda part: lax.all_gather(part, axis), value)  42.7 us
    psum x1, blocking collectives, on_device(): summed_whole = lax.psum(partial_output_value, 'tp')  32.7 us
    all_gather x1, blocking collectives, on_device(): lax.all_gather(qa_part, 'tp', axis=0, tiled=True)  15.8 us
    all_gather x1, blocking collectives, on_device(): lax.all_gather(ob_part, 'tp', axis=1, tiled=True)  15.6 us
    all_gather x1, blocking collectives, on_device(): all_queries = lax.all_gather(query_rows, 'tp', axis=2, tiled=True)  14 us
    all_gather x1, blocking collectives, on_device(): lax.all_gather(query_down_factor, 'group', axis=1, tiled=True)  9.98 us
    all_gather x1, blocking collectives, on_device(): lax.all_gather(output_up_factor, 'group', axis=0, tiled=True)  8.17 us
    all_gather x1, blocking collectives, on_device(): lax.all_gather(query_up_factor, 'group', axis=0, tiled=True)  8.11 us

commit v1 on v0

v1 whole, which is shorter than its diff:
```python
import functools

import jax
import jax.numpy as jnp
from jax import lax
from jax.experimental import pallas as pl
from jax.experimental.pallas import tpu as pltpu
from jax.sharding import PartitionSpec as P

adapter_scale = 2.0
masked_score = -1e30
f32 = jnp.float32
bf16 = jnp.bfloat16
MESH = pl.DeviceIdType.MESH
RANK_TILE = 16
LANES = 128


def rounded_up(value, unit):
    return -(-value // unit) * unit


def dot_nt(a, b):
    return lax.dot_general(a, b, (((1,), (1,)), ((), ())), preferred_element_type=f32)


def dot_nn(a, b):
    return lax.dot_general(a, b, (((1,), (0,)), ((), ())), preferred_element_type=f32)


def dot_wide(a, b):
    rows = a.shape[0]
    one = a.astype(bf16)
    rest = a - one.astype(f32)
    two = rest.astype(bf16)
    three = (rest - two.astype(f32)).astype(bf16)
    parts = dot_nn(jnp.concatenate([one, two, three], axis=0), b)
    return parts[:rows] + (parts[rows : 2 * rows] + parts[2 * rows :])


def pack_rank(value, packed):
    if not packed:
        return value
    half = value.shape[0] // 2
    return jnp.concatenate([value[:half], value[half:]], axis=1)


def unpack_rank(value, packed):
    if not packed:
        return value
    half = value.shape[1] // 2
    return jnp.concatenate([value[:, :half], value[:, half:]], axis=0)


def kernel(
    T,
    G,
    rows,
    steps,
    kv_heads,
    block,
    CW,
    packed,
    x_in,
    wq_in,
    wo_in,
    a_in,
    b_in,
    oa_in,
    ob_in,
    k_in,
    v_in,
    ck_in,
    cv_in,
    len_in,
    out,
    x_v,
    wq_v,
    wo_v,
    a_v,
    oa_v,
    k_v,
    v_v,
    ck_v,
    cv_v,
    len_s,
    at_all,
    b_all,
    u_all,
    r_all,
    oat_all,
    ob_all,
    q_all,
    o_send,
    o_recv,
    rr_all,
    sib_send,
    sib_recv,
    p_send,
    p_recv,
    local_sem,
    tp_send,
    tp_recv,
    g_send,
    g_recv,
    sib_ssem,
    sib_rsem,
    p_ssem,
    p_rsem,
):
    t = lax.axis_index("tp")
    g = lax.axis_index("group")
    R = rows * steps
    chips = T // 2
    core = lax.rem(t, 2)
    chip = lax.div(t, 2)
    sibling = t + 1 - 2 * core
    D = u_all.shape[2]
    gh = T // kv_heads
    scale = D ** (-0.5)

    def local(src, dst, index):
        copy = pltpu.make_async_copy(src, dst, local_sem.at[index])
        copy.start()
        return copy

    load_a = local(a_in, a_v, 0)
    load_oa = local(oa_in, oa_v, 1)
    load_x = local(x_in, x_v, 2)
    load_wq = local(wq_in, wq_v, 3)
    load_b = local(b_in, b_all.at[g, t], 4)
    load_ob = local(ob_in, ob_all.at[g], 5)
    load_k = local(k_in, k_v, 6)
    load_v = local(v_in, v_v, 7)
    load_ck = local(ck_in, ck_v, 8)
    load_cv = local(cv_in, cv_v, 9)
    load_len = local(len_in, len_s, 10)
    load_wo = local(wo_in, wo_v, 11)

    barrier = pltpu.get_barrier_semaphore()
    for d in range(1, T):
        pl.semaphore_signal(
            barrier, inc=1, device_id={"tp": lax.rem(t + d, T)}, device_id_type=MESH
        )
    for e in range(1, G):
        pl.semaphore_signal(
            barrier, inc=1, device_id={"group": lax.rem(g + e, G)}, device_id_type=MESH
        )

    eye = (
        lax.broadcasted_iota(jnp.int32, (RANK_TILE, RANK_TILE), 0)
        == lax.broadcasted_iota(jnp.int32, (RANK_TILE, RANK_TILE), 1)
    ).astype(f32).astype(bf16)
    load_a.wait()
    at_all[g] = dot_nt(eye, a_v[...]).astype(bf16)
    pl.semaphore_wait(barrier, T - 1 + G - 1)

    pending = []

    def over_group(phase, src, dst):
        for e in range(1, G):
            copy = pltpu.make_async_remote_copy(
                src_ref=src,
                dst_ref=dst,
                send_sem=g_send.at[phase, e],
                recv_sem=g_recv.at[phase, e],
                device_id={"group": lax.rem(g + e, G)},
                device_id_type=MESH,
            )
            copy.start()
            pending.append(copy)

    def from_group(phase, slots):
        for e in range(1, G):
            sender = lax.rem(g - e + G, G)
            pltpu.make_async_remote_copy(
                src_ref=slots.at[sender],
                dst_ref=slots.at[sender],
                send_sem=g_send.at[phase, e],
                recv_sem=g_recv.at[phase, e],
                device_id={"group": sender},
                device_id_type=MESH,
            ).wait_recv()

    def over_tp(phase, src, dst):
        for d in range(1, T):
            peer = lax.rem(t + d, T)
            copy = pltpu.make_async_remote_copy(
                src_ref=src(peer),
                dst_ref=dst,
                send_sem=tp_send.at[phase, d],
                recv_sem=tp_recv.at[phase, d],
                device_id={"tp": peer},
                device_id_type=MESH,
            )
            copy.start()
            pending.append(copy)

    def from_tp(phase, slots):
        for d in range(1, T):
            sender = lax.rem(t - d + T, T)
            pltpu.make_async_remote_copy(
                src_ref=slots.at[sender],
                dst_ref=slots.at[sender],
                send_sem=tp_send.at[phase, d],
                recv_sem=tp_recv.at[phase, d],
                device_id={"tp": sender},
                device_id_type=MESH,
            ).wait_recv()

    over_group(0, at_all.at[g], at_all.at[g])
    load_b.wait()
    over_tp(0, lambda peer: b_all.at[g, t], b_all.at[g, t])

    load_x.wait()
    load_wq.wait()
    u_all[t] = dot_nn(x_v[...], wq_v[...])
    over_tp(1, lambda peer: u_all.at[t], u_all.at[t])

    from_group(0, at_all)
    factor = at_all[...].reshape(G * RANK_TILE, CW)
    x_part = x_v[:, pl.ds(pl.multiple_of(t * CW, LANES), CW)]
    r_all[t] = pack_rank(dot_nt(x_part, factor), packed)
    over_tp(2, lambda peer: r_all.at[t], r_all.at[t])

    from_tp(0, b_all.at[g])
    over_group(1, b_all.at[g], b_all.at[g])

    load_oa.wait()
    oat_all[g] = dot_nt(eye, oa_v[...]).astype(bf16)
    load_ob.wait()
    over_group(2, oat_all.at[g], oat_all.at[g])
    over_group(3, ob_all.at[g], ob_all.at[g])

    load_k.wait()
    load_v.wait()
    load_len.wait()
    load_ck.wait()
    load_cv.wait()
    from_tp(1, u_all)
    from_tp(2, r_all)
    rank_inputs = unpack_rank(jnp.sum(r_all[...], axis=0), packed)
    from_group(1, b_all)
    up = jnp.concatenate(
        [
            jnp.concatenate([b_all[i, h] for h in range(T)], axis=1)
            for i in range(G)
        ],
        axis=0,
    )
    adapter = adapter_scale * dot_wide(rank_inputs, up)
    queries = []
    for h in range(T):
        one = (u_all[h] + adapter[:, h * D : (h + 1) * D]).astype(bf16)
        q_all[h] = one
        queries.append(one.astype(f32))

    position = t * block + lax.broadcasted_iota(jnp.int32, (gh * steps, block), 1)
    lane = lax.broadcasted_iota(jnp.int32, (gh * steps, LANES), 1)
    share = LANES // (2 * rows)
    for j in range(kv_heads):
        stat = jnp.zeros((gh * steps, LANES), f32)
        for i in range(rows):
            grouped = jnp.concatenate(
                [
                    queries[h][i * steps : (i + 1) * steps]
                    for h in range(j * gh, (j + 1) * gh)
                ],
                axis=0,
            ).astype(bf16)
            at = (i * kv_heads + j) * block
            scores = dot_nt(grouped, k_v[at : at + block]) * scale
            visible = position < len_s[i]
            peak = jnp.max(
                jnp.where(visible, scores, masked_score), axis=1, keepdims=True
            )
            weights = jnp.where(visible, jnp.exp(scores - peak), 0.0)
            total = jnp.sum(weights, axis=1, keepdims=True)
            outputs = dot_nn(weights.astype(bf16), v_v[at : at + block])
            o_send[j * gh : (j + 1) * gh, i * steps : (i + 1) * steps, :] = (
                outputs.reshape(gh, steps, D)
            )
            stat = jnp.where(
                lane >= 2 * i * share,
                jnp.where(lane >= (2 * i + 1) * share, total, peak),
                stat,
            )
        o_send[j * gh : (j + 1) * gh, R : R + steps, :] = stat.reshape(
            gh, steps, LANES
        )
    over_tp(3, lambda peer: o_send.at[peer], o_recv.at[t])
    o_recv[t] = o_send[t]

    mine = q_all[t]
    fresh_scores = dot_nt(mine, ck_v[...]) * scale
    row_of = lax.broadcasted_iota(jnp.int32, (R, R), 0)
    col_of = lax.broadcasted_iota(jnp.int32, (R, R), 1)
    causal = (lax.div(row_of, steps) == lax.div(col_of, steps)) & (row_of >= col_of)
    fresh_peak = jnp.max(
        jnp.where(causal, fresh_scores, masked_score), axis=1, keepdims=True
    )
    fresh_weights = jnp.where(causal, jnp.exp(fresh_scores - fresh_peak), 0.0)
    fresh_sum = jnp.sum(fresh_weights, axis=1, keepdims=True)
    fresh_out = dot_nn(fresh_weights.astype(bf16), cv_v[...])

    from_group(2, oat_all)
    from_group(3, ob_all)
    load_wo.wait()

    from_tp(3, o_recv)
    stats = o_recv[:, R : R + steps, :]
    peaks, sums, outs = [], [], []
    for i in range(rows):
        block_peak = stats[:, :, 2 * i * share : 2 * i * share + 1]
        block_sum = stats[:, :, (2 * i + 1) * share : (2 * i + 1) * share + 1]
        top = jnp.max(block_peak, axis=0)
        rescale = jnp.exp(block_peak - top[None])
        peaks.append(top)
        sums.append(jnp.sum(rescale * block_sum, axis=0))
        outs.append(
            jnp.sum(rescale * o_recv[:, i * steps : (i + 1) * steps, :], axis=0)
        )
    cache_peak = jnp.concatenate(peaks, axis=0)
    cache_sum = jnp.concatenate(sums, axis=0)
    cache_out = jnp.concatenate(outs, axis=0)
    joint = jnp.maximum(cache_peak, fresh_peak)
    left = jnp.exp(cache_peak - joint)
    right = jnp.exp(fresh_peak - joint)
    numer = cache_out * left + fresh_out * right
    denom = cache_sum * left + fresh_sum * right
    context = (numer / denom).astype(bf16)

    rr_all[t] = pack_rank(
        dot_nt(context, oat_all[...].reshape(G * RANK_TILE, D)), packed
    )

    def columns(device):
        return wo_v[:, pl.ds(pl.multiple_of(device * CW, LANES), CW)]

    order = list(range(1, chips)) + [0]
    to_sibling = {}
    for j in order:
        there = lax.rem(chip + j, chips)
        sib_send[j] = dot_nn(context, columns(2 * there + 1 - core))
        copy = pltpu.make_async_remote_copy(
            src_ref=sib_send.at[j],
            dst_ref=sib_recv.at[j],
            send_sem=sib_ssem.at[j],
            recv_sem=sib_rsem.at[j],
            device_id={"tp": sibling},
            device_id_type=MESH,
        )
        copy.start()
        to_sibling[j] = copy
    over_tp(4, lambda peer: rr_all.at[t], rr_all.at[t])
    for j in order:
        there = lax.rem(chip + j, chips)
        p_send[j] = dot_nn(context, columns(2 * there + core))
    across = {}
    for j in order:
        there = lax.rem(chip + j, chips)
        to_sibling[j].wait_recv()
        p_send[j] += sib_recv[j]
        if j:
            copy = pltpu.make_async_remote_copy(
                src_ref=p_send.at[j],
                dst_ref=p_recv.at[j],
                send_sem=p_ssem.at[j],
                recv_sem=p_rsem.at[j],
                device_id={"tp": 2 * there + core},
                device_id_type=MESH,
            )
            copy.start()
            across[j] = copy
    from_tp(4, rr_all)
    rank_outputs = unpack_rank(jnp.sum(rr_all[...], axis=0), packed)
    result = p_send[0] + adapter_scale * dot_wide(
        rank_outputs, ob_all[...].reshape(G * RANK_TILE, CW)
    )
    for j in range(1, chips):
        across[j].wait_recv()
        result += p_recv[j]
    out[...] = result.astype(out.dtype)

    for copy in pending:
        copy.wait_send()
    for j in order:
        to_sibling[j].wait_send()
        if j:
            across[j].wait_send()


def padded(value, axis, size):
    if value.shape[axis] == size:
        return value
    widths = [(0, 0)] * value.ndim
    widths[axis] = (0, size - value.shape[axis])
    return jnp.pad(value, widths)


def chunked(value, axis, count, size):
    shape = value.shape
    if shape[axis] == count * size:
        return value
    split = shape[:axis] + (count, shape[axis] // count) + shape[axis + 1 :]
    value = padded(value.reshape(split), axis + 1, size)
    return value.reshape(shape[:axis] + (count * size,) + shape[axis + 1 :])


def on_device(
    decoding_input,
    query_weight,
    output_weight,
    query_down_factor,
    query_up_factor,
    output_down_factor,
    output_up_factor,
    stored_keys,
    stored_values,
    current_keys,
    current_values,
    lengths,
):
    T = lax.axis_size("tp")
    G = lax.axis_size("group")
    rows, steps, width = decoding_input.shape
    kv_heads, block, D = stored_keys.shape[1:]
    assert query_weight.shape[1] == D and T % 2 == 0
    R = rows * steps
    chunk = width // T
    CW = rounded_up(chunk, LANES)
    rank = G * RANK_TILE
    packed = 2 * rank == LANES
    rank_shape = (R // 2, LANES) if packed else (R, rank)

    x = chunked(decoding_input.reshape(R, width), 1, T, CW)
    wq = chunked(query_weight, 0, T, CW)
    wo = chunked(output_weight, 1, T, CW)
    a = padded(padded(query_down_factor, 1, RANK_TILE), 0, CW)
    b = padded(query_up_factor, 0, RANK_TILE)
    oa = padded(output_down_factor, 1, RANK_TILE)
    ob = padded(padded(output_up_factor, 0, RANK_TILE), 1, CW)
    k = stored_keys.reshape(rows * kv_heads * block, D)
    v = stored_values.reshape(rows * kv_heads * block, D)
    if kv_heads > 1:
        shared = lax.axis_index("tp") // (T // kv_heads)
        current_keys = lax.dynamic_slice_in_dim(current_keys, shared, 1, 2)
        current_values = lax.dynamic_slice_in_dim(current_values, shared, 1, 2)
    ck = current_keys.reshape(R, D)
    cv = current_values.reshape(R, D)

    vmem = pltpu.VMEM
    dma = pltpu.SemaphoreType.DMA
    result = pl.pallas_call(
        functools.partial(kernel, T, G, rows, steps, kv_heads, block, CW, packed),
        out_shape=jax.ShapeDtypeStruct((R, CW), bf16),
        in_specs=[pl.BlockSpec(memory_space=pl.ANY)] * 12,
        out_specs=pl.BlockSpec(memory_space=pltpu.VMEM),
        scratch_shapes=[
            vmem(x.shape, bf16),
            vmem(wq.shape, bf16),
            vmem(wo.shape, bf16),
            vmem(a.shape, bf16),
            vmem(oa.shape, bf16),
            vmem(k.shape, bf16),
            vmem(v.shape, bf16),
            vmem(ck.shape, bf16),
            vmem(cv.shape, bf16),
            pltpu.SMEM(lengths.shape, jnp.int32),
            vmem((G, RANK_TILE, CW), bf16),
            vmem((G, T, RANK_TILE, D), bf16),
            vmem((T, R, D), f32),
            vmem((T,) + rank_shape, f32),
            vmem((G, RANK_TILE, D), bf16),
            vmem((G, RANK_TILE, CW), bf16),
            vmem((T, R, D), bf16),
            vmem((T, R + steps, D), f32),
            vmem((T, R + steps, D), f32),
            vmem((T,) + rank_shape, f32),
            vmem((T // 2, R, CW), f32),
            vmem((T // 2, R, CW), f32),
            vmem((T // 2, R, CW), f32),
            vmem((T // 2, R, CW), f32),
            dma((12,)),
            dma((5, T)),
            dma((5, T)),
            dma((4, G)),
            dma((4, G)),
            dma((T // 2,)),
            dma((T // 2,)),
            dma((T // 2,)),
            dma((T // 2,)),
        ],
        compiler_params=pltpu.CompilerParams(
            collective_id=0, has_side_effects=True, vmem_limit_bytes=32 * 2**20
        ),
        cost_estimate=pl.CostEstimate(
            flops=4 * R * width * D, bytes_accessed=4 * width * D, transcendentals=0
        ),
    )(x, wq, wo, a, b, oa, ob, k, v, ck, cv, lengths)
    return result[:, :chunk].reshape(rows, steps, chunk)


def solution(mesh):
    in_specs = (
        P("group", None, None),
        P(None, "tp"),
        P("tp", None),
        P("tp", "group"),
        P("group", "tp"),
        P("tp", "group"),
        P("group", "tp"),
        P("group", None, "tp", None),
        P("group", None, "tp", None),
        P("group", None, None, None),
        P("group", None, None, None),
        P("group"),
    )
    out_specs = P("group", None, "tp")
    return jax.shard_map(
        on_device, mesh=mesh, in_specs=in_specs, out_specs=out_specs, check_vma=False
    )
```

time: 161 us -> 38.6 us (0.24)
  blocking collectives: 154 us -> 0 us
  Pallas kernels: 0 us -> 27 us
  local copies, waits for them, and re-layouts: 0.89 us -> 11.1 us
  matrix products: 3.16 us -> 0 us
  other arithmetic: 2.03 us -> 0 us
    all_gather x10 -> x0, blocking collectives: 122 us -> none  [the longest x3 42.7 us: joined(): pieces = jax.tree.map(lambda part: lax.all_gather(part, axis), value)]
    psum x1 -> x0, blocking collectives: 32.7 us -> none  [on_device(): summed_whole = lax.psum(partial_output_value, 'tp')]
    pallas_call x0 -> x1, Pallas kernels: none -> 27 us  [on_device(): pl.pallas_call(functools.partial(kernel, T, G, rows, steps, kv_heads, blo...]
    unnamed x20 -> x23, local copies, waits for them, and re-layouts: 0.06 us -> 11.1 us
    dot_general x10 -> x0, matrix products: 3.16 us -> none  [the longest x1 1.22 us: on_device(): jnp.dot(flattened_input, qa_whole, preferred_element_type=jnp.float32)]
where the time goes in v1:
time: 38.6 us; the launch traced here: 38.1 us
  Pallas kernels  27 us (70%)
  local copies, waits for them, and re-layouts  11.1 us (29%)
    pallas_call x1, Pallas kernels, on_device(): pl.pallas_call(functools.partial(kernel, T, G, rows, steps, kv_heads, blo...  27 us
    unnamed x23, local copies, waits for them, and re-layouts  11.1 us

profile of v1, /device:TPU:0, one launch (start us, length us, event | category | flops | bytes accessed | tf_op | source)
XLA Modules:
  0.0 38.1 jit_solution(825894816393873971)
XLA Ops:
  0.0 0.8 %copy.14.oa_in = bf16[128,16]{1,0:T(8,128)(2,1)S(1)} copy(bf16[128,16]{0,1:T(8,128)(2,1)} %param.17) | data formatting | bytes 8192 | tf_op args[5]
  0.8 0.9 %copy.13.a_in = bf16[640,16]{1,0:T(8,128)(2,1)S(1)} copy(bf16[640,16]{0,1:T(8,128)(2,1)} %param.15) | data formatting | bytes 40960 | tf_op args[3]
  1.7 0.0 copy-start
  1.7 1.3 %copy-done = bf16[5120,128]{1,0:T(8,128)(2,1)S(1)} copy-done((bf16[5120,128]{1,0:T(8,128)(2,1)S(1)}, bf16[5120,128]{1,0:T(8,128)(2,1)}, u32[]{:S(2)}) %copy-start) | copy-done | bytes 1310744
  3.0 0.0 copy-start.1
  3.0 1.3 %copy-done.1 = bf16[128,5120]{1,0:T(8,128)(2,1)S(1)} copy-done((bf16[128,5120]{1,0:T(8,128)(2,1)S(1)}, bf16[128,5120]{1,0:T(8,128)(2,1)}, u32[]{:S(2)}) %copy-start.1) | copy-done | bytes 1310744
  4.3 0.0 copy-start.2
  4.3 0.9 %copy-done.2 = bf16[2,8,5120]{2,1,0:T(8,128)(2,1)S(1)} copy-done((bf16[2,8,5120]{2,1,0:T(8,128)(2,1)S(1)}, bf16[2,8,5120]{2,1,0:T(8,128)(2,1)}, u32[]{:S(2)}) %copy-start.2) | copy-done | bytes 163864
  5.3 0.0 copy-start.3
  5.3 0.9 %copy-done.3 = bf16[2,1,256,128]{3,2,1,0:T(8,128)(2,1)S(1)} copy-done((bf16[2,1,256,128]{3,2,1,0:T(8,128)(2,1)S(1)}, bf16[2,1,256,128]{3,2,1,0:T(8,128)(2,1)}, u32[]{:S(2)}) %copy-start.3) | copy-done | bytes 131096
  6.2 0.0 copy-start.4
  6.2 0.9 %copy-done.4 = bf16[2,1,256,128]{3,2,1,0:T(8,128)(2,1)S(1)} copy-done((bf16[2,1,256,128]{3,2,1,0:T(8,128)(2,1)S(1)}, bf16[2,1,256,128]{3,2,1,0:T(8,128)(2,1)}, u32[]{:S(2)}) %copy-start.4) | copy-done | bytes 131096
  7.1 0.0 copy-start.5
  7.1 0.7 %copy-done.5 = bf16[16,640]{1,0:T(8,128)(2,1)S(1)} copy-done((bf16[16,640]{1,0:T(8,128)(2,1)S(1)}, bf16[16,640]{1,0:T(8,128)(2,1)}, u32[]{:S(2)}) %copy-start.5) | copy-done | bytes 20504
  7.8 0.0 copy-start.6
  7.8 0.7 %copy-done.6 = bf16[16,128]{1,0:T(8,128)(2,1)S(1)} copy-done((bf16[16,128]{1,0:T(8,128)(2,1)S(1)}, bf16[16,128]{1,0:T(8,128)(2,1)}, u32[]{:S(2)}) %copy-start.6) | copy-done | bytes 4120
  8.5 0.0 copy-start.7
  8.5 0.7 %copy-done.7 = bf16[2,8,1,128]{3,1,2,0:T(8,128)(2,1)S(1)} copy-done((bf16[2,8,1,128]{3,1,2,0:T(8,128)(2,1)S(1)}, bf16[2,8,1,128]{3,1,2,0:T(8,128)(2,1)}, u32[]{:S(2)}) %copy-start.7) | copy-done | bytes 4120
  9.2 0.0 copy-start.8
  9.2 0.7 %copy-done.8 = bf16[2,8,1,128]{3,1,2,0:T(8,128)(2,1)S(1)} copy-done((bf16[2,8,1,128]{3,1,2,0:T(8,128)(2,1)S(1)}, bf16[2,8,1,128]{3,1,2,0:T(8,128)(2,1)}, u32[]{:S(2)}) %copy-start.8) | copy-done | bytes 4120
  9.9 0.0 copy-start.9
  9.9 0.7 %copy-done.9 = s32[2]{0:T(128)S(1)} copy-done((s32[2]{0:T(128)S(1)}, s32[2]{0:T(128)}, u32[]{:S(2)}) %copy-start.9) | copy-done | bytes 32
  10.5 27.0 %shard_map.118 = bf16[16,640]{1,0:T(8,128)(2,1)S(1)} custom-call(bf16[16,5120]{1,0:T(8,128)(2,1)S(1)} %bitcast.6, bf16[5120,128]{1,0:T(8,128)(2,1)S(1)} %copy-done, bf16[128,5120]{1,0:T(8,128)(2,1)S(1)} %copy-done.1, bf16[640,16]{1,0:T(8,128)(2,1)S(1)} %copy.13.a_in, bf16[16,128]{1,0:T(8,128)(2,1)S(1)} %copy-done.6, bf16[128,16]{1,0:T(8,128)(2,1)S(1)} %copy.14.oa_in, ...), custom_call_target="tpu_custom_call" | custom-call | flops 41943040 | bytes 2621440 | tf_op jit(solution)/shard_map/pallas_call | solution.py:454
  37.5 0.6 %copy.16 = bf16[2,8,640]{2,1,0:T(8,128)(2,1)} copy(bf16[2,8,640]{2,1,0:T(8,128)(2,1)S(1)} %bitcast.9) | data formatting | bytes 40960
Async XLA Ops:
  1.7 1.3 %copy-start = (bf16[5120,128]{1,0:T(8,128)(2,1)S(1)}, bf16[5120,128]{1,0:T(8,128)(2,1)}, u32[]{:S(2)}) copy-start(bf16[5120,128]{1,0:T(8,128)(2,1)} %wq_in.1) | copy-start | bytes 3932164
  3.0 1.3 %copy-start.1 = (bf16[128,5120]{1,0:T(8,128)(2,1)S(1)}, bf16[128,5120]{1,0:T(8,128)(2,1)}, u32[]{:S(2)}) copy-start(bf16[128,5120]{1,0:T(8,128)(2,1)} %wo_in.1) | copy-start | bytes 3932164
  4.3 0.9 %copy-start.2 = (bf16[2,8,5120]{2,1,0:T(8,128)(2,1)S(1)}, bf16[2,8,5120]{2,1,0:T(8,128)(2,1)}, u32[]{:S(2)}) copy-start(bf16[2,8,5120]{2,1,0:T(8,128)(2,1)} %param.12) | copy-start | bytes 491524
  5.3 0.9 %copy-start.3 = (bf16[2,1,256,128]{3,2,1,0:T(8,128)(2,1)S(1)}, bf16[2,1,256,128]{3,2,1,0:T(8,128)(2,1)}, u32[]{:S(2)}) copy-start(bf16[2,1,256,128]{3,2,1,0:T(8,128)(2,1)} %param.19) | copy-start | bytes 393220
  6.2 0.9 %copy-start.4 = (bf16[2,1,256,128]{3,2,1,0:T(8,128)(2,1)S(1)}, bf16[2,1,256,128]{3,2,1,0:T(8,128)(2,1)}, u32[]{:S(2)}) copy-start(bf16[2,1,256,128]{3,2,1,0:T(8,128)(2,1)} %param.20) | copy-start | bytes 393220
  7.1 0.7 %copy-start.5 = (bf16[16,640]{1,0:T(8,128)(2,1)S(1)}, bf16[16,640]{1,0:T(8,128)(2,1)}, u32[]{:S(2)}) copy-start(bf16[16,640]{1,0:T(8,128)(2,1)} %ob_in.1) | copy-start | bytes 61444
  7.8 0.7 %copy-start.6 = (bf16[16,128]{1,0:T(8,128)(2,1)S(1)}, bf16[16,128]{1,0:T(8,128)(2,1)}, u32[]{:S(2)}) copy-start(bf16[16,128]{1,0:T(8,128)(2,1)} %b_in.1) | copy-start | bytes 12292
  8.5 0.7 %copy-start.7 = (bf16[2,8,1,128]{3,1,2,0:T(8,128)(2,1)S(1)}, bf16[2,8,1,128]{3,1,2,0:T(8,128)(2,1)}, u32[]{:S(2)}) copy-start(bf16[2,8,1,128]{3,1,2,0:T(8,128)(2,1)} %param.21) | copy-start | bytes 12292
  9.2 0.7 %copy-start.8 = (bf16[2,8,1,128]{3,1,2,0:T(8,128)(2,1)S(1)}, bf16[2,8,1,128]{3,1,2,0:T(8,128)(2,1)}, u32[]{:S(2)}) copy-start(bf16[2,8,1,128]{3,1,2,0:T(8,128)(2,1)} %param.22) | copy-start | bytes 12292
  9.9 0.7 %copy-start.9 = (s32[2]{0:T(128)S(1)}, s32[2]{0:T(128)}, u32[]{:S(2)}) copy-start(s32[2]{0:T(128)} %len_in.1) | copy-start | bytes 28

commit v2 on v1

--- a/solution.py
+++ b/solution.py
@@ -77,8 +77,6 @@
     x_v,
     wq_v,
     wo_v,
-    a_v,
-    oa_v,
     k_v,
     v_v,
     ck_v,
@@ -124,8 +122,8 @@
         copy.start()
         return copy
 
-    load_a = local(a_in, a_v, 0)
-    load_oa = local(oa_in, oa_v, 1)
+    load_a = local(a_in, at_all.at[g], 0)
+    load_oa = local(oa_in, oat_all.at[g], 1)
     load_x = local(x_in, x_v, 2)
     load_wq = local(wq_in, wq_v, 3)
     load_b = local(b_in, b_all.at[g, t], 4)
@@ -147,12 +145,7 @@
             barrier, inc=1, device_id={"group": lax.rem(g + e, G)}, device_id_type=MESH
         )
 
-    eye = (
-        lax.broadcasted_iota(jnp.int32, (RANK_TILE, RANK_TILE), 0)
-        == lax.broadcasted_iota(jnp.int32, (RANK_TILE, RANK_TILE), 1)
-    ).astype(f32).astype(bf16)
     load_a.wait()
-    at_all[g] = dot_nt(eye, a_v[...]).astype(bf16)
     pl.semaphore_wait(barrier, T - 1 + G - 1)
 
     pending = []
@@ -227,7 +220,6 @@
     over_group(1, b_all.at[g], b_all.at[g])
 
     load_oa.wait()
-    oat_all[g] = dot_nt(eye, oa_v[...]).astype(bf16)
     load_ob.wait()
     over_group(2, oat_all.at[g], oat_all.at[g])
     over_group(3, ob_all.at[g], ob_all.at[g])
@@ -436,9 +428,9 @@
     x = chunked(decoding_input.reshape(R, width), 1, T, CW)
     wq = chunked(query_weight, 0, T, CW)
     wo = chunked(output_weight, 1, T, CW)
-    a = padded(padded(query_down_factor, 1, RANK_TILE), 0, CW)
+    a = padded(padded(query_down_factor.T, 0, RANK_TILE), 1, CW)
     b = padded(query_up_factor, 0, RANK_TILE)
-    oa = padded(output_down_factor, 1, RANK_TILE)
+    oa = padded(output_down_factor.T, 0, RANK_TILE)
     ob = padded(padded(output_up_factor, 0, RANK_TILE), 1, CW)
     k = stored_keys.reshape(rows * kv_heads * block, D)
     v = stored_values.reshape(rows * kv_heads * block, D)
@@ -454,14 +446,12 @@
     result = pl.pallas_call(
         functools.partial(kernel, T, G, rows, steps, kv_heads, block, CW, packed),
         out_shape=jax.ShapeDtypeStruct((R, CW), bf16),
-        in_specs=[pl.BlockSpec(memory_space=pl.ANY)] * 12,
+        in_specs=[pl.BlockSpec(memory_space=pltpu.HBM)] * 12,
         out_specs=pl.BlockSpec(memory_space=pltpu.VMEM),
         scratch_shapes=[
             vmem(x.shape, bf16),
             vmem(wq.shape, bf16),
             vmem(wo.shape, bf16),
-            vmem(a.shape, bf16),
-            vmem(oa.shape, bf16),
             vmem(k.shape, bf16),
             vmem(v.shape, bf16),
             vmem(ck.shape, bf16),
@@ -492,7 +482,7 @@
             dma((T // 2,)),
         ],
         compiler_params=pltpu.CompilerParams(
-            collective_id=0, has_side_effects=True, vmem_limit_bytes=32 * 2**20
+            collective_id=0, has_side_effects=True, vmem_limit_bytes=56 * 2**20
         ),
         cost_estimate=pl.CostEstimate(
             flops=4 * R * width * D, bytes_accessed=4 * width * D, transcendentals=0

time: 38.6 us -> 28.2 us (0.73)
  local copies, waits for them, and re-layouts: 11.1 us -> 1.34 us
  Pallas kernels: 27 us -> 26.6 us
    unnamed x23 -> x1, local copies, waits for them, and re-layouts: 11.1 us -> 1.34 us
where the time goes in v2:
time: 28.2 us; the launch traced here: 28 us
  Pallas kernels  26.6 us (94%)
  local copies, waits for them, and re-layouts  1.34 us (5%)
    pallas_call x1, Pallas kernels, on_device(): pl.pallas_call(functools.partial(kernel, T, G, rows, steps, kv_heads, blo...  26.6 us
    unnamed x1, local copies, waits for them, and re-layouts  1.34 us

profile of v2, /device:TPU:0, one launch (start us, length us, event | category | flops | bytes accessed | tf_op | source)
XLA Modules:
  0.0 28.0 jit_solution(3470962303321588980)
XLA Ops:
  0.0 26.6 %shard_map.118 = bf16[16,640]{1,0:T(8,128)(2,1)} custom-call(bf16[16,5120]{1,0:T(8,128)(2,1)} %bitcast.8, bf16[5120,128]{1,0:T(8,128)(2,1)} %wq_in.1, bf16[128,5120]{1,0:T(8,128)(2,1)} %wo_in.1, bf16[16,640]{1,0:T(8,128)(2,1)} %bitcast.12, bf16[16,128]{1,0:T(8,128)(2,1)} %b_in.1, bf16[16,128]{1,0:T(8,128)(2,1)} %bitcast.13, bf16[16,640]{1,0:T(8,128)(2,1)} %ob_in.1, ...), custom_call_target="tpu_custom_call" | custom-call | flops 41943040 | bytes 2621440 | tf_op jit(solution)/shard_map/pallas_call | solution.py:446
  26.6 1.3 %copy.14 = bf16[2,8,640]{2,1,0:T(8,128)(2,1)} copy(bf16[2,8,640]{2,1,0:T(8,128)(2,1)} %bitcast.11) | data formatting | bytes 40960

commit v3 on v2

--- a/solution.py
+++ b/solution.py
@@ -36,6 +36,15 @@
     three = (rest - two.astype(f32)).astype(bf16)
     parts = dot_nn(jnp.concatenate([one, two, three], axis=0), b)
     return parts[:rows] + (parts[rows : 2 * rows] + parts[2 * rows :])
+
+
+def partner(index, bits):
+    result, unit = index, 1
+    while unit <= bits:
+        if bits & unit:
+            result = result + unit * (1 - 2 * lax.rem(lax.div(index, unit), 2))
+        unit *= 2
+    return result
 
 
 def pack_rank(value, packed):
@@ -145,7 +154,11 @@
             barrier, inc=1, device_id={"group": lax.rem(g + e, G)}, device_id_type=MESH
         )
 
+    load_x.wait()
+    load_wq.wait()
+    u_all[t] = dot_nn(x_v[...], wq_v[...])
     load_a.wait()
+    load_b.wait()
     pl.semaphore_wait(barrier, T - 1 + G - 1)
 
     pending = []
@@ -176,8 +189,8 @@
             ).wait_recv()
 
     def over_tp(phase, src, dst):
-        for d in range(1, T):
-            peer = lax.rem(t + d, T)
+        for d in reversed(range(1, T)):
+            peer = partner(t, d)
             copy = pltpu.make_async_remote_copy(
                 src_ref=src(peer),
                 dst_ref=dst,
@@ -191,7 +204,7 @@
 
     def from_tp(phase, slots):
         for d in range(1, T):
-            sender = lax.rem(t - d + T, T)
+            sender = partner(t, d)
             pltpu.make_async_remote_copy(
                 src_ref=slots.at[sender],
                 dst_ref=slots.at[sender],
@@ -202,12 +215,8 @@
             ).wait_recv()
 
     over_group(0, at_all.at[g], at_all.at[g])
-    load_b.wait()
     over_tp(0, lambda peer: b_all.at[g, t], b_all.at[g, t])
 
-    load_x.wait()
-    load_wq.wait()
-    u_all[t] = dot_nn(x_v[...], wq_v[...])
     over_tp(1, lambda peer: u_all.at[t], u_all.at[t])
 
     from_group(0, at_all)
@@ -218,11 +227,6 @@
 
     from_tp(0, b_all.at[g])
     over_group(1, b_all.at[g], b_all.at[g])
-
-    load_oa.wait()
-    load_ob.wait()
-    over_group(2, oat_all.at[g], oat_all.at[g])
-    over_group(3, ob_all.at[g], ob_all.at[g])
 
     load_k.wait()
     load_v.wait()
@@ -282,6 +286,10 @@
         )
     over_tp(3, lambda peer: o_send.at[peer], o_recv.at[t])
     o_recv[t] = o_send[t]
+    load_oa.wait()
+    load_ob.wait()
+    over_group(2, oat_all.at[g], oat_all.at[g])
+    over_group(3, ob_all.at[g], ob_all.at[g])
 
     mine = q_all[t]
     fresh_scores = dot_nt(mine, ck_v[...]) * scale
@@ -329,10 +337,10 @@
     def columns(device):
         return wo_v[:, pl.ds(pl.multiple_of(device * CW, LANES), CW)]
 
-    order = list(range(1, chips)) + [0]
+    order = list(reversed(range(chips)))
     to_sibling = {}
     for j in order:
-        there = lax.rem(chip + j, chips)
+        there = partner(chip, j)
         sib_send[j] = dot_nn(context, columns(2 * there + 1 - core))
         copy = pltpu.make_async_remote_copy(
             src_ref=sib_send.at[j],
@@ -346,11 +354,11 @@
         to_sibling[j] = copy
     over_tp(4, lambda peer: rr_all.at[t], rr_all.at[t])
     for j in order:
-        there = lax.rem(chip + j, chips)
+        there = partner(chip, j)
         p_send[j] = dot_nn(context, columns(2 * there + core))
     across = {}
     for j in order:
-        there = lax.rem(chip + j, chips)
+        there = partner(chip, j)
         to_sibling[j].wait_recv()
         p_send[j] += sib_recv[j]
         if j:
@@ -417,7 +425,7 @@
     G = lax.axis_size("group")
     rows, steps, width = decoding_input.shape
     kv_heads, block, D = stored_keys.shape[1:]
-    assert query_weight.shape[1] == D and T % 2 == 0
+    assert query_weight.shape[1] == D and T > 1 and T & (T - 1) == 0
     R = rows * steps
     chunk = width // T
     CW = rounded_up(chunk, LANES)

time: 28.2 us -> 28.6 us (1.014)
  Pallas kernels: 26.6 us -> 27 us
    pallas_call x1, Pallas kernels: 26.6 us -> 27 us  [on_device(): pl.pallas_call(functools.partial(kernel, T, G, rows, steps, kv_heads, blo...]
where the time goes in v3:
time: 28.6 us; the launch traced here: 28.4 us
  Pallas kernels  27 us (94%)
  local copies, waits for them, and re-layouts  1.34 us (5%)
    pallas_call x1, Pallas kernels, on_device(): pl.pallas_call(functools.partial(kernel, T, G, rows, steps, kv_heads, blo...  27 us
    unnamed x1, local copies, waits for them, and re-layouts  1.34 us

profile of v3, /device:TPU:0, one launch (start us, length us, event | category | flops | bytes accessed | tf_op | source)
XLA Modules:
  0.0 28.4 jit_solution(14361588979144487639)
XLA Ops:
  0.0 27.0 %shard_map.118 = bf16[16,640]{1,0:T(8,128)(2,1)} custom-call(bf16[16,5120]{1,0:T(8,128)(2,1)} %bitcast.8, bf16[5120,128]{1,0:T(8,128)(2,1)} %wq_in.1, bf16[128,5120]{1,0:T(8,128)(2,1)} %wo_in.1, bf16[16,640]{1,0:T(8,128)(2,1)} %bitcast.12, bf16[16,128]{1,0:T(8,128)(2,1)} %b_in.1, bf16[16,128]{1,0:T(8,128)(2,1)} %bitcast.13, bf16[16,640]{1,0:T(8,128)(2,1)} %ob_in.1, ...), custom_call_target="tpu_custom_call" | custom-call | flops 41943040 | bytes 2621440 | tf_op jit(solution)/shard_map/pallas_call | solution.py:454
  27.0 1.3 %copy.14 = bf16[2,8,640]{2,1,0:T(8,128)(2,1)} copy(bf16[2,8,640]{2,1,0:T(8,128)(2,1)} %bitcast.11) | data formatting | bytes 40960

commit v4 on v3

--- a/solution.py
+++ b/solution.py
@@ -85,7 +85,7 @@
     out,
     x_v,
     wq_v,
-    wo_v,
+    wo_pair,
     k_v,
     v_v,
     ck_v,
@@ -95,14 +95,14 @@
     b_all,
     u_all,
     r_all,
-    oat_all,
+    oat_pair,
     ob_all,
     q_all,
     o_send,
     o_recv,
-    rr_all,
-    sib_send,
-    sib_recv,
+    rr_own,
+    rr_recv,
+    ctx_pair,
     p_send,
     p_recv,
     local_sem,
@@ -132,7 +132,7 @@
         return copy
 
     load_a = local(a_in, at_all.at[g], 0)
-    load_oa = local(oa_in, oat_all.at[g], 1)
+    load_oa = local(oa_in, oat_pair.at[core, g], 1)
     load_x = local(x_in, x_v, 2)
     load_wq = local(wq_in, wq_v, 3)
     load_b = local(b_in, b_all.at[g, t], 4)
@@ -142,7 +142,13 @@
     load_ck = local(ck_in, ck_v, 8)
     load_cv = local(cv_in, cv_v, 9)
     load_len = local(len_in, len_s, 10)
-    load_wo = local(wo_in, wo_v, 11)
+
+    def columns(device):
+        return wo_in.at[:, pl.ds(pl.multiple_of(device * CW, LANES), CW)]
+
+    load_wo = [
+        local(columns(2 * z + core), wo_pair.at[z, core], 11 + z) for z in range(chips)
+    ]
 
     barrier = pltpu.get_barrier_semaphore()
     for d in range(1, T):
@@ -227,6 +233,31 @@
 
     from_tp(0, b_all.at[g])
     over_group(1, b_all.at[g], b_all.at[g])
+
+    def to_sibling(index, src, dst):
+        copy = pltpu.make_async_remote_copy(
+            src_ref=src,
+            dst_ref=dst,
+            send_sem=sib_ssem.at[index],
+            recv_sem=sib_rsem.at[index],
+            device_id={"tp": sibling},
+            device_id_type=MESH,
+        )
+        copy.start()
+        pending.append(copy)
+
+    def from_sibling(index, slot):
+        pltpu.make_async_remote_copy(
+            src_ref=slot,
+            dst_ref=slot,
+            send_sem=sib_ssem.at[index],
+            recv_sem=sib_rsem.at[index],
+            device_id={"tp": sibling},
+            device_id_type=MESH,
+        ).wait_recv()
+
+    for z in range(chips):
+        to_sibling(z, columns(2 * z + 1 - core), wo_pair.at[z, core])
 
     load_k.wait()
     load_v.wait()
@@ -288,7 +319,7 @@
     o_recv[t] = o_send[t]
     load_oa.wait()
     load_ob.wait()
-    over_group(2, oat_all.at[g], oat_all.at[g])
+    over_group(2, oat_pair.at[core, g], oat_pair.at[core, g])
     over_group(3, ob_all.at[g], ob_all.at[g])
 
     mine = q_all[t]
@@ -303,9 +334,13 @@
     fresh_sum = jnp.sum(fresh_weights, axis=1, keepdims=True)
     fresh_out = dot_nn(fresh_weights.astype(bf16), cv_v[...])
 
-    from_group(2, oat_all)
+    from_group(2, oat_pair.at[core])
+    to_sibling(chips, oat_pair.at[core], oat_pair.at[core])
     from_group(3, ob_all)
-    load_wo.wait()
+    for z in range(chips):
+        load_wo[z].wait()
+        from_sibling(z, wo_pair.at[z, 1 - core])
+    from_sibling(chips, oat_pair.at[1 - core])
 
     from_tp(3, o_recv)
     stats = o_recv[:, R : R + steps, :]
@@ -328,66 +363,53 @@
     right = jnp.exp(fresh_peak - joint)
     numer = cache_out * left + fresh_out * right
     denom = cache_sum * left + fresh_sum * right
-    context = (numer / denom).astype(bf16)
-
-    rr_all[t] = pack_rank(
-        dot_nt(context, oat_all[...].reshape(G * RANK_TILE, D)), packed
-    )
-
-    def columns(device):
-        return wo_v[:, pl.ds(pl.multiple_of(device * CW, LANES), CW)]
-
-    order = list(reversed(range(chips)))
-    to_sibling = {}
-    for j in order:
-        there = partner(chip, j)
-        sib_send[j] = dot_nn(context, columns(2 * there + 1 - core))
+    ctx_pair[core] = (numer / denom).astype(bf16)
+
+    to_sibling(chips + 1, ctx_pair.at[core], ctx_pair.at[core])
+    from_sibling(chips + 1, ctx_pair.at[1 - core])
+    context = jnp.concatenate([ctx_pair[0], ctx_pair[1]], axis=1)
+
+    def across(index, j, src, dst):
         copy = pltpu.make_async_remote_copy(
-            src_ref=sib_send.at[j],
-            dst_ref=sib_recv.at[j],
-            send_sem=sib_ssem.at[j],
-            recv_sem=sib_rsem.at[j],
-            device_id={"tp": sibling},
+            src_ref=src,
+            dst_ref=dst,
+            send_sem=p_ssem.at[index, j],
+            recv_sem=p_rsem.at[index, j],
+            device_id={"tp": 2 * partner(chip, j) + core},
             device_id_type=MESH,
         )
         copy.start()
-        to_sibling[j] = copy
-    over_tp(4, lambda peer: rr_all.at[t], rr_all.at[t])
-    for j in order:
-        there = partner(chip, j)
-        p_send[j] = dot_nn(context, columns(2 * there + core))
-    across = {}
-    for j in order:
-        there = partner(chip, j)
-        to_sibling[j].wait_recv()
-        p_send[j] += sib_recv[j]
+        pending.append(copy)
+        return copy
+
+    arrivals = {}
+    for j in reversed(range(chips)):
+        p_send[j] = dot_nn(context, wo_pair[partner(chip, j)].reshape(2 * D, CW))
         if j:
-            copy = pltpu.make_async_remote_copy(
-                src_ref=p_send.at[j],
-                dst_ref=p_recv.at[j],
-                send_sem=p_ssem.at[j],
-                recv_sem=p_rsem.at[j],
-                device_id={"tp": 2 * there + core},
-                device_id_type=MESH,
-            )
-            copy.start()
-            across[j] = copy
-    from_tp(4, rr_all)
-    rank_outputs = unpack_rank(jnp.sum(rr_all[...], axis=0), packed)
+            arrivals[j] = across(0, j, p_send.at[j], p_recv.at[j])
+    rr_own[...] = pack_rank(
+        dot_nt(ctx_pair[0], oat_pair[0].reshape(G * RANK_TILE, D))
+        + dot_nt(ctx_pair[1], oat_pair[1].reshape(G * RANK_TILE, D)),
+        packed,
+    )
+    ranks = {}
+    for j in reversed(range(1, chips)):
+        ranks[j] = across(1, j, rr_own, rr_recv.at[j])
+    rank_sum = rr_own[...]
+    for j in range(1, chips):
+        ranks[j].wait_recv()
+        rank_sum += rr_recv[j]
+    rank_outputs = unpack_rank(rank_sum, packed)
     result = p_send[0] + adapter_scale * dot_wide(
         rank_outputs, ob_all[...].reshape(G * RANK_TILE, CW)
     )
     for j in range(1, chips):
-        across[j].wait_recv()
+        arrivals[j].wait_recv()
         result += p_recv[j]
     out[...] = result.astype(out.dtype)
 
     for copy in pending:
         copy.wait_send()
-    for j in order:
-        to_sibling[j].wait_send()
-        if j:
-            across[j].wait_send()
 
 
 def padded(value, axis, size):
@@ -453,13 +475,13 @@
     dma = pltpu.SemaphoreType.DMA
     result = pl.pallas_call(
         functools.partial(kernel, T, G, rows, steps, kv_heads, block, CW, packed),
-        out_shape=jax.ShapeDtypeStruct((R, CW), bf16),
+        out_shape=pltpu.VMEM((R, CW), bf16),
         in_specs=[pl.BlockSpec(memory_space=pltpu.HBM)] * 12,
         out_specs=pl.BlockSpec(memory_space=pltpu.VMEM),
         scratch_shapes=[
             vmem(x.shape, bf16),
             vmem(wq.shape, bf16),
-            vmem(wo.shape, bf16),
+            vmem((T // 2, 2, D, CW), bf16),
             vmem(k.shape, bf16),
             vmem(v.shape, bf16),
             vmem(ck.shape, bf16),
@@ -469,25 +491,25 @@
             vmem((G, T, RANK_TILE, D), bf16),
             vmem((T, R, D), f32),
             vmem((T,) + rank_shape, f32),
-            vmem((G, RANK_TILE, D), bf16),
+            vmem((2, G, RANK_TILE, D), bf16),
             vmem((G, RANK_TILE, CW), bf16),
             vmem((T, R, D), bf16),
             vmem((T, R + steps, D), f32),
             vmem((T, R + steps, D), f32),
-            vmem((T,) + rank_shape, f32),
+            vmem(rank_shape, f32),
+            vmem((T // 2,) + rank_shape, f32),
+            vmem((2, R, D), bf16),
             vmem((T // 2, R, CW), f32),
             vmem((T // 2, R, CW), f32),
-            vmem((T // 2, R, CW), f32),
-            vmem((T // 2, R, CW), f32),
-            dma((12,)),
-            dma((5, T)),
-            dma((5, T)),
+            dma((11 + T // 2,)),
+            dma((4, T)),
+            dma((4, T)),
             dma((4, G)),
             dma((4, G)),
-            dma((T // 2,)),
-            dma((T // 2,)),
-            dma((T // 2,)),
-            dma((T // 2,)),
+            dma((T // 2 + 2,)),
+            dma((T // 2 + 2,)),
+            dma((2, T // 2)),
+            dma((2, T // 2)),
         ],
         compiler_params=pltpu.CompilerParams(
             collective_id=0, has_side_effects=True, vmem_limit_bytes=56 * 2**20

time: 28.6 us -> 27.3 us (0.955)
  local copies, waits for them, and re-layouts: 1.34 us -> 0.61 us
  Pallas kernels: 27 us -> 26.5 us
    unnamed x1, local copies, waits for them, and re-layouts: 1.34 us -> 0.61 us
    pallas_call x1, Pallas kernels: 27 us -> 26.5 us  [on_device(): pl.pallas_call(functools.partial(kernel, T, G, rows, steps, kv_heads, blo...]
where the time goes in v4:
time: 27.3 us; the launch traced here: 27.1 us
  Pallas kernels  26.5 us (97%)
  local copies, waits for them, and re-layouts  0.61 us (2%)
    pallas_call x1, Pallas kernels, on_device(): pl.pallas_call(functools.partial(kernel, T, G, rows, steps, kv_heads, blo...  26.5 us
    unnamed x1, local copies, waits for them, and re-layouts  0.61 us

profile of v4, /device:TPU:0, one launch (start us, length us, event | category | flops | bytes accessed | tf_op | source)
XLA Modules:
  0.0 27.1 jit_solution(8594429667127179485)
XLA Ops:
  0.0 26.5 %shard_map.118 = bf16[16,640]{1,0:T(8,128)(2,1)S(1)} custom-call(bf16[16,5120]{1,0:T(8,128)(2,1)} %bitcast.9, bf16[5120,128]{1,0:T(8,128)(2,1)} %wq_in.1, bf16[128,5120]{1,0:T(8,128)(2,1)} %wo_in.1, bf16[16,640]{1,0:T(8,128)(2,1)} %bitcast.12, bf16[16,128]{1,0:T(8,128)(2,1)} %b_in.1, bf16[16,128]{1,0:T(8,128)(2,1)} %bitcast.13, bf16[16,640]{1,0:T(8,128)(2,1)} %ob_in.1, ...), custom_call_target="tpu_custom_call" | custom-call | flops 41943040 | bytes 2621440 | tf_op jit(solution)/shard_map/pallas_call | solution.py:476
  26.5 0.6 %copy.14 = bf16[2,8,640]{2,1,0:T(8,128)(2,1)} copy(bf16[2,8,640]{2,1,0:T(8,128)(2,1)S(1)} %bitcast.8) | data formatting | bytes 40960

commit v5 on v4

--- a/solution.py
+++ b/solution.py
@@ -382,11 +382,6 @@
         pending.append(copy)
         return copy
 
-    arrivals = {}
-    for j in reversed(range(chips)):
-        p_send[j] = dot_nn(context, wo_pair[partner(chip, j)].reshape(2 * D, CW))
-        if j:
-            arrivals[j] = across(0, j, p_send.at[j], p_recv.at[j])
     rr_own[...] = pack_rank(
         dot_nt(ctx_pair[0], oat_pair[0].reshape(G * RANK_TILE, D))
         + dot_nt(ctx_pair[1], oat_pair[1].reshape(G * RANK_TILE, D)),
@@ -395,6 +390,14 @@
     ranks = {}
     for j in reversed(range(1, chips)):
         ranks[j] = across(1, j, rr_own, rr_recv.at[j])
+    arrivals = {}
+    for j in reversed(range(chips)):
+        p_send[j] = dot_nn(context, wo_pair[partner(chip, j)].reshape(2 * D, CW))
+        if j:
+            arrivals[j] = across(0, j, p_send.at[j], p_recv.at[j])
+    last = 2 * (chips - 1)
+    for copy in pending[: len(pending) - last]:
+        copy.wait_send()
     rank_sum = rr_own[...]
     for j in range(1, chips):
         ranks[j].wait_recv()
@@ -408,7 +411,7 @@
         result += p_recv[j]
     out[...] = result.astype(out.dtype)
 
-    for copy in pending:
+    for copy in pending[len(pending) - last :]:
         copy.wait_send()
 
 

time: 27.3 us -> 27.1 us (level)
  no operation moved by 1% of the time
where the time goes in v5:
time: 27.1 us; the launch traced here: 26.9 us
  Pallas kernels  26.3 us (97%)
  local copies, waits for them, and re-layouts  0.61 us (2%)
    pallas_call x1, Pallas kernels, on_device(): pl.pallas_call(functools.partial(kernel, T, G, rows, steps, kv_heads, blo...  26.3 us
    unnamed x1, local copies, waits for them, and re-layouts  0.61 us

profile of v5, /device:TPU:0, one launch (start us, length us, event | category | flops | bytes accessed | tf_op | source)
XLA Modules:
  0.0 26.9 jit_solution(15168890911595404739)
XLA Ops:
  0.0 26.3 %shard_map.118 = bf16[16,640]{1,0:T(8,128)(2,1)S(1)} custom-call(bf16[16,5120]{1,0:T(8,128)(2,1)} %bitcast.9, bf16[5120,128]{1,0:T(8,128)(2,1)} %wq_in.1, bf16[128,5120]{1,0:T(8,128)(2,1)} %wo_in.1, bf16[16,640]{1,0:T(8,128)(2,1)} %bitcast.12, bf16[16,128]{1,0:T(8,128)(2,1)} %b_in.1, bf16[16,128]{1,0:T(8,128)(2,1)} %bitcast.13, bf16[16,640]{1,0:T(8,128)(2,1)} %ob_in.1, ...), custom_call_target="tpu_custom_call" | custom-call | flops 41943040 | bytes 2621440 | tf_op jit(solution)/shard_map/pallas_call | solution.py:479
  26.3 0.6 %copy.14 = bf16[2,8,640]{2,1,0:T(8,128)(2,1)} copy(bf16[2,8,640]{2,1,0:T(8,128)(2,1)S(1)} %bitcast.8) | data formatting | bytes 40960
